TPU v7x, 32 devices: a whole 2x2x4 slice. The times are simulated.
32 devices in a mesh: sec: 2 (over core), gx: 4 (over z), gy: 4 (over y, x).
Axes of the slice: x: 2, y: 2, z: 4, core: 2. Of those that a mesh axis runs over, the one named last changes fastest.
Arguments:
- air_sea_state: float32 [2, 16, 192, 1024], P('sec', None, 'gx', 'gy'), may hold values from -6 to 6
- diffusion: float32 [2, 16], P('sec'), may hold values from 0.04 to 0.15
- courant: float32 [2, 16], P('sec'), may hold values from 0.1 to 0.35
- exchange_coef: float32 [2, 192, 1024], P('sec', 'gx', 'gy'), may hold values from 0.2 to 1
- src_block: int32 [2, 3072], P('sec', ('gx', 'gy')), may hold values from 0 to 95
- dest_peer: int32 [2, 3072, 1], P('sec', ('gx', 'gy')), may hold values from 0 to 15; in each aligned block of 192 rows (0 to 191, 192 to 383, ..., all dimensions but the last counted through in order) at most 24 rows name the same one
- dest_block: int32 [2, 3072], P('sec', ('gx', 'gy')), may hold values from 0 to 95
- remap_weight: float32 [2, 3072, 128, 128], P('sec', ('gx', 'gy')), may hold values from -0.375 to 0.375
Outputs:
- new_state: float32 [2, 16, 192, 1024], P('sec', None, 'gx', 'gy')
- remapped: float32 [2, 4, 192, 1024], P('sec', None, 'gx', 'gy')
Inputs may be any that keep to these rules, and one draw needn't show every extreme that they name: `dest_peer`: among the 192 entries owned by one device (aligned blocks of 192 entries of one component), no destination device is named more than 24 times, and in every draw some device is named exactly 24 times by some owner.
All inputs are finite; a program needn't handle non-finite values.
Results may differ from a plain program's by a relative error of at most 0.0001.
Values sent between devices are 32-bit elements; how exact they have to be, the bound alone decides.
A program may use at most 64 MiB of HBM per device.

v0:
```python
import functools

import jax
import jax.numpy as jnp
from jax import lax
from jax.experimental import pallas as pl
from jax.experimental.pallas import tpu as pltpu
from jax.sharding import PartitionSpec as P

NF = 4
BLK = 128
STEPS_A = 6
STEPS_O = 3
HALO = 8
CHUNKS = 8
MESH = pl.DeviceIdType.MESH
F32 = jnp.float32
BF16 = jnp.bfloat16
SIDES = ((1, 0), (-1, 0), (0, 1), (0, -1), (1, 1), (1, -1), (-1, 1), (-1, -1))


def split_2(value):
    high = value.astype(BF16)
    return high, (value - high.astype(F32)).astype(BF16)


def dot_t(a, b):
    return lax.dot_general(a, b, (((1,), (1,)), ((), ())), preferred_element_type=F32)


def kernel(
    grid_x, grid_y, cap,
    state_hbm, diff_hbm, cour_hbm, coef_hbm, src_hbm, peer_hbm, block_hbm, w_hbm,
    new_state, remapped,
    state, diff, cour, coef, src_row, peer_row, block_row,
    w_f32, w_parts, rows_after, rows_before, edge_right, edge_left, cols_before, cols_after,
    inside, surf, table, take, picked, prods, pick, outgoing, incoming, lab_out, lab_in, spread, total,
    in_sem, w_sem, halo_send, halo_recv, high_send, high_recv, lab_send, lab_recv, out_send, out_recv,
):
    sec, gx, gy = lax.axis_index("sec"), lax.axis_index("gx"), lax.axis_index("gy")
    peers = grid_x * grid_y
    me = gx * grid_y + gy
    levels, rows, cols = state.shape
    entries = peer_row.shape[1]
    blocks = rows * (cols // BLK)
    slots = peers * cap
    rows_ext, cols_ext = rows + 2 * HALO, cols + BLK
    per_chunk = entries * BLK // CHUNKS

    def w_copy(c):
        part = pl.ds(c * per_chunk, per_chunk)
        return pltpu.make_async_copy(w_hbm.at[part], w_f32.at[part], w_sem.at[c])

    small = [
        pltpu.make_async_copy(source, dest, in_sem.at[i])
        for i, (source, dest) in enumerate((
            (state_hbm, state), (peer_hbm, peer_row), (block_hbm, block_row), (src_hbm, src_row),
            (diff_hbm, diff), (cour_hbm, cour), (coef_hbm, coef),
        ))
    ]
    for copy in small:
        copy.start()
    for c in range(CHUNKS):
        w_copy(c).start()

    def there(side):
        dx, dy = side
        ok = jnp.bool_(True)
        if dx:
            ok = (gx < grid_x - 1) if dx > 0 else (gx > 0)
        if dy:
            ok_y = (gy < grid_y - 1) if dy > 0 else (gy > 0)
            ok = jnp.logical_and(ok, ok_y) if dx else ok_y
        return ok

    barrier = pltpu.get_barrier_semaphore()
    count = jnp.int32(peers)
    for dx, dy in SIDES:
        ok = there((dx, dy))
        count = count + jnp.where(ok, 1, 0)

        @pl.when(ok)
        def _(dx=dx, dy=dy):
            pl.semaphore_signal(
                barrier, inc=1, device_id=(sec, gx + dx, gy + dy), device_id_type=MESH
            )

    def other(k):
        p = lax.rem(me + k, peers)
        return p, (1 - sec, p // grid_y, lax.rem(p, grid_y))

    @pl.loop(0, peers)
    def _(k):
        pl.semaphore_signal(barrier, inc=1, device_id=other(k)[1], device_id_type=MESH)

    shape_ext = (rows_ext, cols_ext)
    r = lax.broadcasted_iota(jnp.int32, shape_ext, 0)
    c = lax.broadcasted_iota(jnp.int32, shape_ext, 1)
    r = jnp.where(r < rows + HALO, r, r - rows_ext) + gx * rows
    near = (c < cols + HALO) | (c >= cols_ext - HALO)
    c = jnp.where(c < cols + HALO, c, c - cols_ext) + gy * cols
    ok = near & (r >= 0) & (r < grid_x * rows) & (c >= 0) & (c < grid_y * cols)
    inside[...] = jnp.where(ok, 1.0, 0.0)

    for copy in small[1:]:
        copy.wait()

    dest_row = peer_row[...].astype(F32)
    square = (entries, entries)
    e_row = lax.broadcasted_iota(jnp.int32, square, 1)
    e_col = lax.broadcasted_iota(jnp.int32, square, 0)
    wide = jnp.broadcast_to(dest_row, square)
    dest_col = jnp.sum(jnp.where(e_row == e_col, wide, 0.0), axis=1, keepdims=True)
    earlier = jnp.where((dest_col == wide) & (e_col < e_row), 1.0, 0.0)
    rank_row = jnp.sum(earlier, axis=0, keepdims=True)
    slot_row = (dest_row * cap + rank_row).astype(jnp.int32)
    pick[...] = jnp.where(
        lax.broadcasted_iota(jnp.int32, (slots, entries), 0) == slot_row, 1.0, 0.0
    ).astype(BF16)
    number = block_row[...]
    label = ((number % 2) * (blocks // 2) + number // 2 + 1).astype(F32)
    peer_at = lax.broadcasted_iota(jnp.int32, (peers, entries), 0)
    rank_at = lax.broadcasted_iota(jnp.int32, (BLK, entries), 0)
    source = src_row[...]
    source = ((source % 2) * (blocks // 2) + source // 2).astype(F32)
    source = jnp.sum(
        jnp.where(e_row == e_col, jnp.broadcast_to(source, square), 0.0), axis=1, keepdims=True
    )
    block_at = lax.broadcasted_iota(jnp.int32, (entries, blocks), 1)
    take[...] = jnp.where(block_at == source.astype(jnp.int32), 1.0, 0.0).astype(BF16)
    of_peer = jnp.where(peer_at == peer_row[...], label, 0.0).astype(BF16)
    of_rank = jnp.where(rank_at == rank_row.astype(jnp.int32), 1.0, 0.0).astype(BF16)
    labels = dot_t(of_peer, of_rank)
    lab_out[...] = jnp.broadcast_to(labels[:, None, :], lab_out.shape)

    small[0].wait()

    lane = lax.broadcasted_iota(jnp.int32, (rows, BLK), 1)

    def pack(l, carry):
        right, left = carry
        hit = (lane >= l * HALO) & (lane < l * HALO + HALO)
        last = state[l, :, cols - BLK :]
        first = state[l, :, :BLK]
        right = jnp.where(hit, pltpu.roll(last, l * HALO + HALO, 1), right)
        left = jnp.where(hit, pltpu.roll(first, l * HALO, 1), left)
        return right, left

    zero = jnp.zeros((rows, BLK), F32)
    right, left = (zero, zero)
    for l in range(levels):
        right, left = pack(l, (right, left))
    edge_right[...] = right
    edge_left[...] = left

    top, bottom = pl.ds(rows - HALO, HALO), pl.ds(0, HALO)
    below, above = pl.ds(rows, HALO), pl.ds(rows + HALO, HALO)
    low, high = pl.ds(0, NF), pl.ds(NF, levels - NF)
    everything = pl.ds(0, rows)
    ends = {
        (1, 0): (state.at[low, top], rows_before.at[low]),
        (-1, 0): (state.at[low, bottom], rows_after.at[low]),
        (0, 1): (edge_right.at[everything], cols_before.at[everything]),
        (0, -1): (edge_left.at[everything], cols_after.at[everything]),
        (1, 1): (edge_right.at[top], cols_before.at[above]),
        (1, -1): (edge_left.at[top], cols_after.at[above]),
        (-1, 1): (edge_right.at[bottom], cols_before.at[below]),
        (-1, -1): (edge_left.at[bottom], cols_after.at[below]),
    }
    for dx, dy in SIDES:
        dest = ends[dx, dy][1]

        @pl.when(jnp.logical_not(there((-dx, -dy))))
        def _(dx=dx, dy=dy, dest=dest):
            dest[...] = jnp.zeros(dest.shape, F32)
            if (dx, dy) == (1, 0):
                rows_before[NF:] = jnp.zeros((levels - NF, HALO, cols), F32)
            if (dx, dy) == (-1, 0):
                rows_after[NF:] = jnp.zeros((levels - NF, HALO, cols), F32)

    pl.semaphore_wait(barrier, count)

    def halo_copy(i):
        dx, dy = SIDES[i]
        source, dest = ends[dx, dy]
        return pltpu.make_async_remote_copy(
            src_ref=source, dst_ref=dest, send_sem=halo_send.at[i], recv_sem=halo_recv.at[i],
            device_id=(sec, gx + dx, gy + dy), device_id_type=MESH,
        )

    def high_copy(i):
        dx, dy = SIDES[i]
        source, dest = ((state.at[high, top], rows_before.at[high]),
                        (state.at[high, bottom], rows_after.at[high]))[i]
        return pltpu.make_async_remote_copy(
            src_ref=source, dst_ref=dest, send_sem=high_send.at[i], recv_sem=high_recv.at[i],
            device_id=(sec, gx + dx, gy + dy), device_id_type=MESH,
        )

    for i, side in enumerate(SIDES):
        pl.when(there(side))(lambda i=i: halo_copy(i).start())

    def lab_copy(p, target, slot):
        return pltpu.make_async_remote_copy(
            src_ref=lab_out.at[p], dst_ref=lab_in.at[slot],
            send_sem=lab_send.at[p], recv_sem=lab_recv.at[slot],
            device_id=target, device_id_type=MESH,
        )

    def out_copy(p, target, slot):
        return pltpu.make_async_remote_copy(
            src_ref=outgoing.at[p], dst_ref=incoming.at[slot],
            send_sem=out_send.at[p], recv_sem=out_recv.at[slot],
            device_id=target, device_id_type=MESH,
        )

    @pl.loop(0, peers)
    def _(k):
        p, target = other(k)
        lab_copy(p, target, me).start()

    for i, side in enumerate(SIDES[:2]):
        pl.when(there(side))(lambda i=i: high_copy(i).start())

    for chunk in range(CHUNKS):
        w_copy(chunk).wait()

        @pl.loop(0, per_chunk // BLK)
        def _(t, chunk=chunk):
            at = pl.ds(pl.multiple_of(chunk * per_chunk + t * BLK, BLK), BLK)
            part_high, part_low = split_2(w_f32[at, :])
            w_parts[at, :BLK] = part_high
            w_parts[at, BLK:] = part_low

    steps = jnp.where(sec == 0, STEPS_A, STEPS_O)
    side_lane = lax.broadcasted_iota(jnp.int32, (rows_ext, BLK), 1)

    def run(l):
        before = pltpu.roll(cols_before[...], BLK - HALO - l * HALO, 1)
        after = pltpu.roll(cols_after[...], lax.rem(BLK - l * HALO, BLK), 1)
        beside = jnp.where(
            side_lane < HALO, after, jnp.where(side_lane >= BLK - HALO, before, 0.0)
        )
        middle = jnp.concatenate([state[l], rows_after[l], rows_before[l]], axis=0)
        u = jnp.concatenate([middle, beside], axis=1)
        diffuse, carry_rate = diff[0, l], cour[0, l]

        def step(_, u):
            prev_x = pltpu.roll(u, 1, 0)
            around = (
                pltpu.roll(u, rows_ext - 1, 0) + prev_x
                + pltpu.roll(u, cols_ext - 1, 1) + pltpu.roll(u, 1, 1)
            )
            return u + inside[...] * (
                diffuse * (around - 4.0 * u) - carry_rate * (u - prev_x)
            )

        return lax.fori_loop(0, steps, step, u)[:rows, :cols]

    for i, (dx, dy) in enumerate(SIDES):
        pl.when(there((-dx, -dy)))(lambda i=i: halo_copy(i).wait_recv())

    for f in range(NF):
        u = run(jnp.int32(f))
        surf[f] = u
        part_high, part_low = split_2(u)
        for h in range(cols // BLK):
            at = slice(h * BLK, (h + 1) * BLK)
            of_block = slice(h * rows, (h + 1) * rows)
            table[of_block, f * BLK : (f + 1) * BLK] = part_high[:, at]
            table[of_block, (f + NF) * BLK : (f + NF + 1) * BLK] = part_low[:, at]

    gathered = jnp.dot(take[...], table[...], preferred_element_type=F32)
    for f in range(2 * NF):
        picked[pl.ds(f, entries, stride=2 * NF), :] = gathered[:, f * BLK : (f + 1) * BLK]

    @pl.loop(0, entries // 2, unroll=16)
    def _(g):
        left = picked[pl.ds(pl.multiple_of(g * 16, 16), 16), :].astype(BF16)
        left = jnp.concatenate([left, left], axis=1)
        out = dot_t(left, w_parts[pl.ds(pl.multiple_of(g * 2 * BLK, 2 * BLK), 2 * BLK), :])
        at = pl.multiple_of(g * 16, 16)
        prods[pl.ds(at, 8), :] = out[:8, :BLK]
        prods[pl.ds(at + 8, 8), :] = out[8:, BLK:]

    parts = []
    for f in range(NF):
        whole = prods[pl.ds(f, entries, stride=8), :] + prods[pl.ds(f + NF, entries, stride=8), :]
        parts.append(split_2(whole))
    both = jnp.concatenate([p for p, _ in parts] + [p for _, p in parts], axis=1)
    group = slots // grid_x

    @pl.loop(0, grid_x)
    def _(k):
        g = lax.rem(gx // 2 + 1 + k // 2, grid_x // 2) * 2 + lax.rem(gx + k, 2)
        chosen = pick[pl.ds(pl.multiple_of(g * group, 16), group), :]
        found = jnp.dot(chosen, both, preferred_element_type=F32)
        for f in range(NF):
            value = found[:, f * BLK : (f + 1) * BLK] + found[:, (f + NF) * BLK : (f + NF + 1) * BLK]
            outgoing[pl.ds(g * grid_y, grid_y), f] = value.reshape(grid_y, cap, BLK)

        @pl.loop(0, grid_y)
        def _(j):
            to_y = lax.rem(gy + j, grid_y)
            out_copy(g * grid_y + to_y, (1 - sec, g, to_y), me).start()

    for i, (dx, dy) in enumerate(SIDES[:2]):
        pl.when(there((-dx, -dy)))(lambda i=i: high_copy(i).wait_recv())

    @pl.loop(NF, levels)
    def _(l):
        new_state[l] = run(l)

    @pl.loop(0, peers)
    def _(k):
        p, target = other(k)
        lab_copy(p, target, p).wait_recv()

    in_cap = lax.rem(lax.broadcasted_iota(jnp.int32, (group, BLK), 0), cap)
    own = lax.broadcasted_iota(jnp.int32, (group, BLK), 1) == in_cap
    rows_at = lax.broadcasted_iota(jnp.int32, (blocks, group), 0) + 1

    @pl.loop(0, grid_x)
    def _(g):
        tall = lab_in[pl.ds(g * grid_y, grid_y)]
        tall = jnp.concatenate([tall] * (cap // 8), axis=1).reshape(group, BLK)
        label_at = dot_t(jnp.ones((blocks, BLK), BF16), jnp.where(own, tall, 0.0).astype(BF16))
        spread[g] = jnp.where(label_at.astype(jnp.int32) == rows_at, 1.0, 0.0).astype(BF16)

    total[...] = jnp.zeros(total.shape, F32)

    @pl.loop(0, grid_x)
    def _(k):
        g = lax.rem(gx // 2 + k // 2, grid_x // 2) * 2 + lax.rem(gx + k, 2)

        @pl.loop(0, grid_y)
        def _(j):
            out_copy(g * grid_y + j, (1 - sec, g, j), g * grid_y + j).wait_recv()

        came = incoming[pl.ds(g * grid_y, grid_y)]
        parts = [split_2(came[:, f].reshape(group, BLK)) for f in range(NF)]
        both = jnp.concatenate([p for p, _ in parts] + [p for _, p in parts], axis=1)
        added = jnp.dot(spread[g], both, preferred_element_type=F32)
        total[...] += added[:, : NF * BLK] + added[:, NF * BLK :]

    for f in range(NF):
        for h in range(cols // BLK):
            at = slice(h * BLK, (h + 1) * BLK)
            value = total[h * rows : (h + 1) * rows, f * BLK : (f + 1) * BLK]
            remapped[f, :, at] = value
            now = surf[f, :, at]
            new_state[f, :, at] = now + coef[:, at] * jnp.tanh(value - now)

    for i, side in enumerate(SIDES):
        pl.when(there(side))(lambda i=i: halo_copy(i).wait_send())
    for i, side in enumerate(SIDES[:2]):
        pl.when(there(side))(lambda i=i: high_copy(i).wait_send())

    @pl.loop(0, peers)
    def _(k):
        p, target = other(k)
        lab_copy(p, target, me).wait_send()
        out_copy(p, target, me).wait_send()


def body(
    air_sea_state, diffusion, courant, exchange_coef, src_block, dest_peer, dest_block, remap_weight
):
    _, levels, rows, cols = air_sea_state.shape
    entries = remap_weight.shape[1]
    grid_x, grid_y = lax.axis_size("gx"), lax.axis_size("gy")
    peers = grid_x * grid_y
    cap = -(-max(2, 2 * entries // peers) // 8) * 8
    slots = peers * cap
    blocks = rows * (cols // BLK)
    vmem = pl.BlockSpec(memory_space=pltpu.VMEM)
    dma = pltpu.SemaphoreType.DMA
    new_state, remapped = pl.pallas_call(
        functools.partial(kernel, grid_x, grid_y, cap),
        name="coupled_interval",
        out_shape=(
            jax.ShapeDtypeStruct((levels, rows, cols), F32),
            jax.ShapeDtypeStruct((NF, rows, cols), F32),
        ),
        in_specs=[pl.BlockSpec(memory_space=pltpu.HBM)] * 8,
        out_specs=(vmem, vmem),
        scratch_shapes=[
            pltpu.VMEM((levels, rows, cols), F32),
            pltpu.SMEM((1, levels), F32),
            pltpu.SMEM((1, levels), F32),
            pltpu.VMEM((rows, cols), F32),
            pltpu.VMEM((1, entries), jnp.int32),
            pltpu.VMEM((1, entries), jnp.int32),
            pltpu.VMEM((1, entries), jnp.int32),
            pltpu.VMEM((entries * BLK, BLK), F32),
            pltpu.VMEM((entries * BLK, 2 * BLK), BF16),
            pltpu.VMEM((levels, HALO, cols), F32),
            pltpu.VMEM((levels, HALO, cols), F32),
            pltpu.VMEM((rows, BLK), F32),
            pltpu.VMEM((rows, BLK), F32),
            pltpu.VMEM((rows + 2 * HALO, BLK), F32),
            pltpu.VMEM((rows + 2 * HALO, BLK), F32),
            pltpu.VMEM((rows + 2 * HALO, cols + BLK), F32),
            pltpu.VMEM((NF, rows, cols), F32),
            pltpu.VMEM((blocks, 2 * NF * BLK), BF16),
            pltpu.VMEM((entries, blocks), BF16),
            pltpu.VMEM((entries * 2 * NF, BLK), F32),
            pltpu.VMEM((entries * 2 * NF, BLK), F32),
            pltpu.VMEM((slots, entries), BF16),
            pltpu.VMEM((peers, NF, cap, BLK), F32),
            pltpu.VMEM((peers, NF, cap, BLK), F32),
            pltpu.VMEM((peers, 8, BLK), F32),
            pltpu.VMEM((peers, 8, BLK), F32),
            pltpu.VMEM((grid_x, blocks, slots // grid_x), BF16),
            pltpu.VMEM((blocks, NF * BLK), F32),
            dma((7,)),
            dma((CHUNKS,)),
            dma((len(SIDES),)), dma((len(SIDES),)),
            dma((2,)), dma((2,)),
            dma((peers,)), dma((peers,)),
            dma((peers,)), dma((peers,)),
        ],
        compiler_params=pltpu.CompilerParams(
            collective_id=0, has_side_effects=True, vmem_limit_bytes=60 * 1024 * 1024
        ),
    )(
        air_sea_state[0],
        diffusion,
        courant,
        exchange_coef[0],
        src_block,
        dest_peer[:, :, 0],
        dest_block,
        remap_weight.reshape(entries * BLK, BLK),
    )
    return new_state[None], remapped[None]


def solution(mesh):
    in_specs = (
        P("sec", None, "gx", "gy"),
        P("sec", None),
        P("sec", None),
        P("sec", "gx", "gy"),
        P("sec", ("gx", "gy")),
        P("sec", ("gx", "gy"), None),
        P("sec", ("gx", "gy")),
        P("sec", ("gx", "gy"), None, None),
    )
    out_specs = (P("sec", None, "gx", "gy"), P("sec", None, "gx", "gy"))
    return jax.shard_map(body, mesh=mesh, in_specs=in_specs, out_specs=out_specs, check_vma=False)
```

profile of v0, /device:TPU:11, one launch (start us, length us, event | category | flops | bytes accessed | tf_op | source)
XLA Modules:
  0.0 42.0 jit_solution(1956823698903171415)
XLA Ops:
  0.6 37.7 %coupled_interval.1 = (f32[16,48,256]{2,1,0:T(8,128)}, f32[4,48,256]{2,1,0:T(8,128)}) custom-call(f32[16,48,256]{2,1,0:T(8,128)} %bitcast.7, f32[1,16]{1,0:T(1,128)} %diff_hbm.1, f32[1,16]{1,0:T(1,128)} %cour_hbm.1, f32[48,256]{1,0:T(8,128)} %bitcast.10, s32[1,192]{1,0:T(1,128)} %src_hbm.1, s32[1,192]{1,0:T(1,128)} %bitcast.11, s32[1,192]{1,0:T(1,128)} %block_hbm.1, ...), custom_call_target="tpu_custom_call" | custom-call | tf_op jit(solution)/shard_map/coupled_interval/pallas_call | solution.py:378
  38.4 2.1 %copy.12 = f32[1,16,48,256]{3,2,1,0:T(8,128)} copy(f32[1,16,48,256]{3,2,1,0:T(8,128)} %bitcast.8) | data formatting | bytes 1572864
  40.4 1.6 %copy.13 = f32[1,4,48,256]{3,2,1,0:T(8,128)} copy(f32[1,4,48,256]{3,2,1,0:T(8,128)} %bitcast.9) | data formatting | bytes 393216
where the time goes:
time: 42.2 us; the launch traced here: 42 us
  Pallas kernels  37.7 us (89%)
  local copies, waits for them, and re-layouts  3.68 us (9%)
  between operations  0.64 us (2%)
    pallas_call x1, Pallas kernels, body(): pl.pallas_call(functools.partial(kernel, grid_x, grid_y, cap), name='coup...  37.7 us
    unnamed x2, local copies, waits for them, and re-layouts  3.68 us

commit v1 on v0

--- a/solution.py
+++ b/solution.py
@@ -30,12 +30,12 @@
 
 def kernel(
     grid_x, grid_y, cap,
-    state_hbm, diff_hbm, cour_hbm, coef_hbm, src_hbm, peer_hbm, block_hbm, w_hbm,
-    new_state, remapped,
-    state, diff, cour, coef, src_row, peer_row, block_row,
+    state_hbm, diff_hbm, cour_hbm, src_hbm, peer_hbm, block_hbm, w_hbm,
+    surface_hbm, aloft_hbm, sum_high, sum_low,
+    state, diff, cour, src_row, peer_row, block_row,
     w_f32, w_parts, rows_after, rows_before, edge_right, edge_left, cols_before, cols_after,
-    inside, surf, table, take, picked, prods, pick, outgoing, incoming, lab_out, lab_in, spread, total,
-    in_sem, w_sem, halo_send, halo_recv, high_send, high_recv, lab_send, lab_recv, out_send, out_recv,
+    inside, stepped, table, take, picked, prods, pick, outgoing, incoming, lab_out, lab_in, spread, total,
+    in_sem, step_sem, w_sem, halo_send, halo_recv, high_send, high_recv, lab_send, lab_recv, out_send, out_recv,
 ):
     sec, gx, gy = lax.axis_index("sec"), lax.axis_index("gx"), lax.axis_index("gy")
     peers = grid_x * grid_y
@@ -55,7 +55,7 @@
         pltpu.make_async_copy(source, dest, in_sem.at[i])
         for i, (source, dest) in enumerate((
             (state_hbm, state), (peer_hbm, peer_row), (block_hbm, block_row), (src_hbm, src_row),
-            (diff_hbm, diff), (cour_hbm, cour), (coef_hbm, coef),
+            (diff_hbm, diff), (cour_hbm, cour),
         ))
     ]
     for copy in small:
@@ -225,7 +225,7 @@
     for chunk in range(CHUNKS):
         w_copy(chunk).wait()
 
-        @pl.loop(0, per_chunk // BLK)
+        @pl.loop(0, per_chunk // BLK, unroll=4)
         def _(t, chunk=chunk):
             at = pl.ds(pl.multiple_of(chunk * per_chunk + t * BLK, BLK), BLK)
             part_high, part_low = split_2(w_f32[at, :])
@@ -262,7 +262,7 @@
 
     for f in range(NF):
         u = run(jnp.int32(f))
-        surf[f] = u
+        stepped[f] = u
         part_high, part_low = split_2(u)
         for h in range(cols // BLK):
             at = slice(h * BLK, (h + 1) * BLK)
@@ -309,7 +309,14 @@
 
     @pl.loop(NF, levels)
     def _(l):
-        new_state[l] = run(l)
+        stepped[l] = run(l)
+
+    keep = (
+        pltpu.make_async_copy(stepped.at[low], surface_hbm, step_sem.at[0]),
+        pltpu.make_async_copy(stepped.at[high], aloft_hbm, step_sem.at[1]),
+    )
+    for copy in keep:
+        copy.start()
 
     @pl.loop(0, peers)
     def _(k):
@@ -341,16 +348,17 @@
         parts = [split_2(came[:, f].reshape(group, BLK)) for f in range(NF)]
         both = jnp.concatenate([p for p, _ in parts] + [p for _, p in parts], axis=1)
         added = jnp.dot(spread[g], both, preferred_element_type=F32)
-        total[...] += added[:, : NF * BLK] + added[:, NF * BLK :]
+        total[...] += added
 
     for f in range(NF):
         for h in range(cols // BLK):
             at = slice(h * BLK, (h + 1) * BLK)
-            value = total[h * rows : (h + 1) * rows, f * BLK : (f + 1) * BLK]
-            remapped[f, :, at] = value
-            now = surf[f, :, at]
-            new_state[f, :, at] = now + coef[:, at] * jnp.tanh(value - now)
-
+            of_block = slice(h * rows, (h + 1) * rows)
+            sum_high[f, :, at] = total[of_block, f * BLK : (f + 1) * BLK]
+            sum_low[f, :, at] = total[of_block, (f + NF) * BLK : (f + NF + 1) * BLK]
+
+    for copy in keep:
+        copy.wait()
     for i, side in enumerate(SIDES):
         pl.when(there(side))(lambda i=i: halo_copy(i).wait_send())
     for i, side in enumerate(SIDES[:2]):
@@ -375,20 +383,21 @@
     blocks = rows * (cols // BLK)
     vmem = pl.BlockSpec(memory_space=pltpu.VMEM)
     dma = pltpu.SemaphoreType.DMA
-    new_state, remapped = pl.pallas_call(
+    surface, aloft, sum_high, sum_low = pl.pallas_call(
         functools.partial(kernel, grid_x, grid_y, cap),
         name="coupled_interval",
         out_shape=(
-            jax.ShapeDtypeStruct((levels, rows, cols), F32),
+            jax.ShapeDtypeStruct((NF, rows, cols), F32),
+            jax.ShapeDtypeStruct((levels - NF, rows, cols), F32),
+            jax.ShapeDtypeStruct((NF, rows, cols), F32),
             jax.ShapeDtypeStruct((NF, rows, cols), F32),
         ),
-        in_specs=[pl.BlockSpec(memory_space=pltpu.HBM)] * 8,
-        out_specs=(vmem, vmem),
+        in_specs=[pl.BlockSpec(memory_space=pltpu.HBM)] * 7,
+        out_specs=(pl.BlockSpec(memory_space=pltpu.HBM), pl.BlockSpec(memory_space=pltpu.HBM), vmem, vmem),
         scratch_shapes=[
             pltpu.VMEM((levels, rows, cols), F32),
             pltpu.SMEM((1, levels), F32),
             pltpu.SMEM((1, levels), F32),
-            pltpu.VMEM((rows, cols), F32),
             pltpu.VMEM((1, entries), jnp.int32),
             pltpu.VMEM((1, entries), jnp.int32),
             pltpu.VMEM((1, entries), jnp.int32),
@@ -401,7 +410,7 @@
             pltpu.VMEM((rows + 2 * HALO, BLK), F32),
             pltpu.VMEM((rows + 2 * HALO, BLK), F32),
             pltpu.VMEM((rows + 2 * HALO, cols + BLK), F32),
-            pltpu.VMEM((NF, rows, cols), F32),
+            pltpu.VMEM((levels, rows, cols), F32),
             pltpu.VMEM((blocks, 2 * NF * BLK), BF16),
             pltpu.VMEM((entries, blocks), BF16),
             pltpu.VMEM((entries * 2 * NF, BLK), F32),
@@ -412,8 +421,9 @@
             pltpu.VMEM((peers, 8, BLK), F32),
             pltpu.VMEM((peers, 8, BLK), F32),
             pltpu.VMEM((grid_x, blocks, slots // grid_x), BF16),
-            pltpu.VMEM((blocks, NF * BLK), F32),
-            dma((7,)),
+            pltpu.VMEM((blocks, 2 * NF * BLK), F32),
+            dma((6,)),
+            dma((2,)),
             dma((CHUNKS,)),
             dma((len(SIDES),)), dma((len(SIDES),)),
             dma((2,)), dma((2,)),
@@ -427,12 +437,14 @@
         air_sea_state[0],
         diffusion,
         courant,
-        exchange_coef[0],
         src_block,
         dest_peer[:, :, 0],
         dest_block,
         remap_weight.reshape(entries * BLK, BLK),
     )
+    remapped = sum_high + sum_low
+    surface = surface + exchange_coef * jnp.tanh(remapped - surface)
+    new_state = jnp.concatenate([surface, aloft], axis=0)
     return new_state[None], remapped[None]
 
 

time: 42.2 us -> 41.3 us (0.979)
  other arithmetic: 0 us -> 3.83 us
  local copies, waits for them, and re-layouts: 3.68 us -> 0.01 us
  Pallas kernels: 37.7 us -> 36.6 us
    broadcast_in_dim x0 -> x2, other arithmetic: none -> 3.83 us  [body(): return (new_state[None], remapped[None])]
    unnamed x2, local copies, waits for them, and re-layouts: 3.68 us -> 0.01 us
    pallas_call x1, Pallas kernels: 37.7 us -> 36.6 us  [body(): pl.pallas_call(functools.partial(kernel, grid_x, grid_y, cap), name='coup...]
where the time goes in v1:
time: 41.3 us; the launch traced here: 41.1 us
  Pallas kernels  36.6 us (89%)
  other arithmetic  3.83 us (9%)
  between operations  0.66 us (2%)
    pallas_call x1, Pallas kernels, body(): pl.pallas_call(functools.partial(kernel, grid_x, grid_y, cap), name='coup...  36.6 us
    broadcast_in_dim x2, other arithmetic, body(): return (new_state[None], remapped[None])  3.83 us

profile of v1, /device:TPU:11, one launch (start us, length us, event | category | flops | bytes accessed | tf_op | source)
XLA Modules:
  0.0 41.1 jit_solution(2337690092452243916)
XLA Ops:
  0.6 0.0 copy-start
  0.6 36.6 %coupled_interval.1 = (f32[4,48,256]{2,1,0:T(8,128)}, f32[12,48,256]{2,1,0:T(8,128)}, f32[4,48,256]{2,1,0:T(8,128)}, f32[4,48,256]{2,1,0:T(8,128)}) custom-call(f32[16,48,256]{2,1,0:T(8,128)} %bitcast.9, f32[1,16]{1,0:T(1,128)} %diff_hbm.1, f32[1,16]{1,0:T(1,128)} %cour_hbm.1, s32[1,192]{1,0:T(1,128)} %src_hbm.1, s32[1,192]{1,0:T(1,128)} %bitcast.11, ...), custom_call_target="tpu_custom_call" | custom-call | tf_op jit(solution)/shard_map/coupled_interval/pallas_call | solution.py:386
  37.2 0.0 copy-done
  37.3 1.8 %add_bitcast_fusion = (f32[1,4,48,256]{3,2,1,0:T(8,128)}, f32[4,48,256]{2,1,0:T(8,128)S(1)}) fusion(f32[4,48,256]{2,1,0:T(8,128)} %get-tuple-element.7, f32[4,48,256]{2,1,0:T(8,128)} %get-tuple-element.8, f32[4,48,256]{2,1,0:T(8,128)} %get-tuple-element.6, f32[48,256]{1,0:T(8,128)S(1)} %bitcast.10), kind=kLoop, calls=%fused_computation.2 | loop fusion | flops 196608 | bytes 1032192 | tf_op jit(solution)/shard_map/broadcast_in_dim | solution.py:448
  39.1 2.0 %maximum_bitcast_fusion = f32[1,16,48,256]{3,2,1,0:T(8,128)} fusion(f32[12,48,256]{2,1,0:T(8,128)} %get-tuple-element.9, f32[4,48,256]{2,1,0:T(8,128)S(1)} %get-tuple-element.11), kind=kLoop, calls=%fused_computation | loop fusion | flops 196608 | bytes 1572864 | tf_op jit(solution)/shard_map/broadcast_in_dim | solution.py:448
Async XLA Ops:
  0.6 36.6 %copy-start = (f32[1,48,256]{2,1,0:T(8,128)S(1)}, f32[1,48,256]{2,1,0:T(8,128)}, u32[]{:S(2)}) copy-start(f32[1,48,256]{2,1,0:T(8,128)} %param.11) | copy-start | bytes 147460
